TPU v7x, 256 devices: a whole 4x4x8 slice. The times are simulated.
256 devices in a mesh: dp: 32 (over y_hi, z, core), mp: 8 (over x, y_lo).
Axes of the slice: x: 4, y: 4 (y_hi: 2, y_lo: 2; y = y_hi * 2 + y_lo), z: 8, core: 2. Of those that a mesh axis runs over, the one named last changes fastest.
Arguments:
- features: bfloat16 [32768, 4096], P('dp'), may hold values from -13 to 13
- out_grads: bfloat16 [32768, 4096], P('dp', 'mp'), may hold values from -6 to 6
- counts: int32 [32], P('dp'), may hold values from 341 to 1024, as said below
- factor_old: float32 [8, 32, 2, 512, 512], P('mp', 'dp'), may hold values from -1 to 3, as said below
- inverse_old: float32 [8, 32, 2, 512, 512], P('mp', 'dp'), may hold values from -1 to 3, as said below
- old_owner: int32 [8, 2], replicated, may hold values from 0 to 31, as said below
- new_owner: int32 [8, 2], replicated, may hold values from 0 to 31, as said below
Outputs:
- factor_new: float32 [8, 32, 512, 512], P('mp', 'dp')
- inverse_new: float32 [8, 32, 512, 512], P('mp', 'dp')
- update: float32 [4096, 4096], P('dp', 'mp')
Inputs may be any that keep to these rules, and one draw needn't show every extreme that they name: `counts`: some dp index has all 1024 rows valid. `factor_old`: Symmetric. `inverse_old`: Symmetric. `old_owner`: A dp index holds at most both blocks of one mp index; in every draw some mp index has both blocks at one dp index. `new_owner`: the two blocks of one mp index have different new owners.
All inputs are finite; a program needn't handle non-finite values.
Results may differ from a plain program's by a relative error of at most 0.0057.
Values may be sent and summed in bfloat16 or wider, within the bound.
No kernel may reach another device: no remote copies, remote signals or barrier semaphores. Data moves between devices by JAX's collectives and lax.ppermute only.
A program may use at most 128 MiB of HBM per device.

v0:
```python
import jax
import jax.numpy as jnp
from jax import lax
from jax.sharding import PartitionSpec as P

DECAY = 0.9
DAMPING = 0.01


def from_root(block, axis, owner):
    block = jnp.where(lax.axis_index(axis) == owner, block, jnp.zeros_like(block))
    return lax.psum(block, axis)


def contract_rows(first_rows, second_rows):
    return lax.dot_general(
        first_rows, second_rows, (((0,), (0,)), ((), ())), preferred_element_type=jnp.float32
    )


def refresh(stale_factor, stale_inverse, covariance, token_total):
    block_width = stale_factor.shape[0]
    factor = DECAY * stale_factor + (1.0 - DECAY) * covariance / token_total
    damped = factor + DAMPING * jnp.eye(block_width, dtype=jnp.float32)
    inner_prod = jnp.dot(damped, stale_inverse, precision=lax.Precision.HIGHEST)
    inverse = 2.0 * stale_inverse - jnp.dot(
        stale_inverse, inner_prod, precision=lax.Precision.HIGHEST
    )
    return (factor, inverse)


def local(features, out_grads, counts, factor_old, inverse_old, old_owner, new_owner):
    block_width = out_grads.shape[1]
    tok_rows = features.shape[0]
    feature_count = features.shape[1]
    column = lax.axis_index("mp")
    member = lax.axis_index("dp")
    members = lax.axis_size("dp")
    valid_rows = (jnp.arange(tok_rows, dtype=jnp.int32) < counts[0])[:, None]
    grads_kept = jnp.where(valid_rows, out_grads, jnp.zeros_like(out_grads))
    own_block = lax.dynamic_slice_in_dim(features, column * block_width, block_width, 1)
    block_kept = jnp.where(valid_rows, own_block, jnp.zeros_like(own_block))
    partials = jnp.stack(
        [contract_rows(block_kept, own_block), contract_rows(grads_kept, out_grads)]
    )
    summed, totals = lax.psum((partials, counts.astype(jnp.float32)), "dp")
    token_total = totals[0]
    stale_owner = lax.dynamic_index_in_dim(old_owner, column, 0, keepdims=False)
    fresh_owner = lax.dynamic_index_in_dim(new_owner, column, 0, keepdims=False)
    shared_slot = (stale_owner[1] == stale_owner[0]).astype(jnp.int32)
    slot_index = (jnp.zeros((), jnp.int32), shared_slot)
    held_factors = factor_old[0, 0]
    held_inverses = inverse_old[0, 0]
    blank_block = jnp.zeros((block_width, block_width), jnp.float32)
    factor_out = blank_block
    inverse_out = blank_block
    rounded = []
    for which_block in range(2):
        stale_factor = lax.dynamic_index_in_dim(
            held_factors, slot_index[which_block], 0, keepdims=False
        )
        stale_inverse = lax.dynamic_index_in_dim(
            held_inverses, slot_index[which_block], 0, keepdims=False
        )
        covariance = summed[which_block]
        factor, inverse = lax.cond(
            member == stale_owner[which_block],
            lambda: refresh(stale_factor, stale_inverse, covariance, token_total),
            lambda: (blank_block, blank_block),
        )
        both_blocks = from_root(jnp.stack([factor, inverse]), "dp", stale_owner[which_block])
        factor = both_blocks[0]
        inverse = both_blocks[1]
        rounded.append(inverse.astype(jnp.bfloat16))
        keeper = member == fresh_owner[which_block]
        factor_out = jnp.where(keeper, factor, factor_out)
        inverse_out = jnp.where(keeper, inverse, inverse_out)
    right_inverse = rounded[1]
    left_inverses = lax.all_gather(rounded[0][None], "mp", axis=0, tiled=True)
    share_rows = block_width // members
    summed_grad = lax.psum_scatter(
        contract_rows(grads_kept, features), "dp", scatter_dimension=0, tiled=True
    )
    grad_round = summed_grad.astype(jnp.bfloat16)
    stacked = grad_round.reshape(share_rows, -1, block_width)
    half_step = jnp.einsum(
        "hck,cik->hci", stacked, left_inverses, preferred_element_type=jnp.float32
    )
    half_step = half_step.reshape(share_rows, feature_count).astype(jnp.bfloat16)
    half_moved, grad_moved = (
        lax.all_to_all(half_step, "dp", split_axis=1, concat_axis=0, tiled=True),
        lax.all_to_all(grad_round, "dp", split_axis=1, concat_axis=0, tiled=True),
    )
    result_turned = contract_rows(right_inverse, half_moved)
    curvature = jnp.sum(result_turned * grad_moved.astype(jnp.float32))
    result = result_turned.T
    curvature = lax.psum(curvature, ("dp", "mp"))
    entries = float(feature_count * block_width * lax.axis_size("mp"))
    clip_scale = jnp.minimum(1.0, jnp.sqrt(entries / jnp.abs(curvature)))
    return (factor_out[None, None], inverse_out[None, None], clip_scale * result)


def solution(mesh):
    return jax.shard_map(
        local,
        mesh=mesh,
        in_specs=(
            P("dp", None),
            P("dp", "mp"),
            P("dp"),
            P("mp", "dp", None, None, None),
            P("mp", "dp", None, None, None),
            P(),
            P(),
        ),
        out_specs=(P("mp", "dp", None, None), P("mp", "dp", None, None), P("dp", "mp")),
        check_vma=False,
    )
```

profile of v0, /device:TPU:1, one launch (start us, length us, event | category | flops | bytes accessed | tf_op | source)
XLA Modules:
  0.0 956.5 jit_solution(16445997575437055482)
XLA Ops:
  7.9 2.4 fusion.39
  10.3 2.4 fusion.42
  12.7 1.6 pad_maximum_fusion
  14.3 70.3 %psum.36 = f32[]{:T(128)} all-reduce(f32[]{:T(128)} %bitcast.12), channel_id=1, replica_groups=mesh['dp'=32,'mp'=8] {'dp'}, use_global_device_ids=true, to_apply=%region_1.2 | all-reduce | flops 1 | bytes 8 | tf_op jit(solution)/shard_map/psum | solution.py:46
  87.8 201.8 %all-reduce.4.cloned.1.call-done = f32[2,512,512]{2,1,0:T(8,128)} async-done(((f32[2,512,512]{2,1,0:T(8,128)}), f32[2,512,512]{2,1,0:T(8,128)}) %all-reduce.4.cloned.1.call-update) | async-done | bytes 2097168 | tf_op jit(solution)/shard_map/psum | solution.py:46
  289.6 1.2 conditional.3
  289.7 1.1 stack.31.clone
  290.8 2.8 maximum_select_fusion.1
  293.6 1.2 conditional.2
  293.8 1.1 stack.29.clone
  294.9 2.8 maximum_select_fusion
  297.9 1.0 copy-done.4
  298.9 10.3 %fusion.35 = f32[512,4096]{1,0:T(8,128)} fusion(bf16[1024,4096]{1,0:T(8,128)(2,1)} %param.11, bf16[1024,512]{1,0:T(8,128)(2,1)S(1)} %copy-done.4, pred[1024]{0:T(1024)(128)(4,1)S(1)} %iota_compare_fusion.4), kind=kOutput, calls=%fused_computation.50 | convolution fusion | flops 4295491584 | bytes 17826816 | tf_op jit(solution)/shard_map/dot_general | solution.py:16
  309.3 286.9 %all-reduce.6.cloned.1.call-done = (f32[2,512,512]{2,1,0:T(8,128)}, f32[2,512,512]{2,1,0:T(8,128)}) async-done(((f32[2,512,512]{2,1,0:T(8,128)}, f32[2,512,512]{2,1,0:T(8,128)}), (f32[2,512,512]{2,1,0:T(8,128)}, f32[2,512,512]{2,1,0:T(8,128)})) %all-reduce.6.cloned.1.call-update) | async-done | bytes 4194320 | tf_op jit(solution)/shard_map/psum | solution.py:12
  596.1 2.1 slice.84
  600.1 149.4 %reduce-scatter.2.cloned.1.call-done = f32[16,4096]{1,0:T(8,128)} async-done(((f32[512,4096]{1,0:T(8,128)}), f32[16,4096]{1,0:T(8,128)}) %reduce-scatter.2.cloned.1.call-update) | async-done | bytes 262160 | tf_op jit(solution)/shard_map/reduce_scatter | solution.py:81
  749.5 1.6 copy_bitcast_fusion
  751.1 10.9 %all-to-all-start.1 = ((bf16[16,32,128]{2,0,1:T(8,128)(2,1)}), bf16[16,32,128]{2,0,1:T(8,128)(2,1)S(1)}, u32[]{:S(2)}, u32[]{:S(2)}) async-start(bf16[16,32,128]{2,0,1:T(8,128)(2,1)} %copy_bitcast_fusion), calls=%async_computation.2 | async-start | bytes 262144 | tf_op jit(solution)/shard_map/all_to_all | solution.py:92
  763.0 84.6 %all-gather.2.cloned.1.call-done = bf16[8,512,512]{2,1,0:T(8,128)(2,1)} async-done(((bf16[1,512,512]{2,1,0:T(8,128)(2,1)}), bf16[8,512,512]{2,1,0:T(8,128)(2,1)}) %all-gather.2.cloned.1.call-update) | async-done | bytes 4194320 | tf_op jit(solution)/shard_map/all_gather | solution.py:79
  847.6 3.5 fusion.45
  852.0 9.2 all-to-all-start
  861.3 3.4 select_bitcast_fusion
  864.6 7.2 all-to-all-done
  872.8 75.6 %psum.39 = f32[]{:T(128)} all-reduce(f32[]{:T(128)} %get-tuple-element.140), channel_id=1, replica_groups=mesh['dp'=32,'mp'=8] {'dp','mp'}, use_global_device_ids=true, to_apply=%region_10.11 | all-reduce | flops 1 | bytes 8 | tf_op jit(solution)/shard_map/psum | solution.py:97
  (31 shorter events, 5.4 us)
Async XLA Ops:
  7.2 282.4 %all-reduce.4.cloned.1.call-start = ((), (), s32[]{:S(2)}) async-start(), calls=%async_computation.3 | async-start | bytes 4194304 | tf_op jit(solution)/shard_map/psum | solution.py:46
  14.3 70.3 %copy-start.5 = (s32[8,2]{0,1:T(2,128)S(1)}, s32[8,2]{0,1:T(2,128)}, u32[]{:S(2)}) copy-start(s32[8,2]{0,1:T(2,128)} %param.16) | copy-start | bytes 196
  14.3 70.3 %copy-start.6 = (s32[8,2]{0,1:T(2,128)S(1)}, s32[8,2]{0,1:T(2,128)}, u32[]{:S(2)}) copy-start(s32[8,2]{0,1:T(2,128)} %param.17) | copy-start | bytes 196
  14.3 275.3 %copy-start = (f32[1,1,2,512,512]{4,3,2,1,0:T(8,128)S(1)}, f32[1,1,2,512,512]{4,3,2,1,0:T(8,128)}, u32[]{:S(2)}) copy-start(f32[1,1,2,512,512]{4,3,2,1,0:T(8,128)} %param.15) | copy-start | bytes 6291460
  14.3 581.9 %all-reduce.6.cloned.1.call-start = ((), (), s32[]{:S(2)}) async-start(), calls=%async_computation.6 | async-start | bytes 8388608 | tf_op jit(solution)/shard_map/psum | solution.py:12
  297.7 1.2 copy-start.4
  297.7 451.8 %reduce-scatter.2.cloned.1.call-start = ((), (), s32[]{:S(2)}) async-start(), calls=%async_computation.5 | async-start | bytes 8650752 | tf_op jit(solution)/shard_map/reduce_scatter | solution.py:81
  309.2 538.3 %all-gather.2.cloned.1.call-start = ((), (), s32[]{:S(2)}) async-start(), calls=%async_computation.4 | async-start | bytes 4718592 | tf_op jit(solution)/shard_map/all_gather | solution.py:79
  751.1 100.9 %all-to-all-start.1 = ((bf16[16,32,128]{2,0,1:T(8,128)(2,1)}), bf16[16,32,128]{2,0,1:T(8,128)(2,1)S(1)}, u32[]{:S(2)}, u32[]{:S(2)}) async-start(bf16[16,32,128]{2,0,1:T(8,128)(2,1)} %copy_bitcast_fusion), calls=%async_computation.2 | async-start | bytes 262144 | tf_op jit(solution)/shard_map/all_to_all | solution.py:92
  847.6 13.7 %copy-start.2 = (f32[2,512,512]{2,1,0:T(8,128)S(1)}, f32[2,512,512]{2,1,0:T(8,128)}, u32[]{:S(2)}) copy-start(f32[2,512,512]{2,1,0:T(8,128)} %get-tuple-element.133) | copy-start | bytes 6291460
  852.0 19.8 %all-to-all-start = ((bf16[16,32,128]{2,0,1:T(8,128)(2,1)}), bf16[16,32,128]{2,0,1:T(8,128)(2,1)S(1)}, u32[]{:S(2)}, u32[]{:S(2)}) async-start(bf16[16,32,128]{2,0,1:T(8,128)(2,1)} %copy.29), calls=%async_computation.1 | async-start | bytes 262144 | tf_op jit(solution)/shard_map/all_to_all | solution.py:91
Sparse Core Ops, SparseCore 0:
  14.4 275.1 all-reduce.3
  297.8 298.2 all-reduce.5
  601.2 148.2 reduce-scatter.1
  751.8 95.7 all-gather.1
where the time goes:
time: 957 us; the launch traced here: 956 us
  waiting for transfers between devices  730 us (76%)
  blocking collectives  146 us (15%)
  starting transfers between devices  20.5 us (2%)
  matrix products  19.6 us (2%)
  between operations  19.1 us (2%)
  other arithmetic  13.1 us (1%)
    psum x1, waiting for transfers between devices, from_root(): return lax.psum(block, axis)  287 us
    psum x1, waiting for transfers between devices, local(): summed, totals = lax.psum((partials, counts.astype(jnp.float32)), 'dp')  202 us
    reduce_scatter x1, waiting for transfers between devices, local(): lax.psum_scatter(contract_rows(grads_kept, features), 'dp', scatter_dimen...  149 us
    all_gather x1, waiting for transfers between devices, local(): left_inverses = lax.all_gather(rounded[0][None], 'mp', axis=0, tiled=True)  84.6 us
    psum x1, blocking collectives, local(): curvature = lax.psum(curvature, ('dp', 'mp'))  75.6 us
    psum x1, blocking collectives, local(): summed, totals = lax.psum((partials, counts.astype(jnp.float32)), 'dp')  70.3 us
  transfers between devices with their start and end apart: 6, of which 5 were waited for; matrix products, arithmetic and copies ran while one was open for 2% of the time, Pallas kernels for 0%

commit v1 on v0

--- a/solution.py
+++ b/solution.py
@@ -76,7 +76,15 @@
         factor_out = jnp.where(keeper, factor, factor_out)
         inverse_out = jnp.where(keeper, inverse, inverse_out)
     right_inverse = rounded[1]
-    left_inverses = lax.all_gather(rounded[0][None], "mp", axis=0, tiled=True)
+    left_inverses = jnp.concatenate(
+        lax.all_to_all(
+            jnp.stack(lax.axis_size("mp") * [rounded[0][None]]),
+            axis_name="mp",
+            split_axis=0,
+            concat_axis=0,
+        ),
+        axis=0,
+    )
     share_rows = block_width // members
     summed_grad = lax.psum_scatter(
         contract_rows(grads_kept, features), "dp", scatter_dimension=0, tiled=True

time: 957 us -> 874 us (0.913)
  waiting for transfers between devices: 730 us -> 645 us
    all_gather x1 -> x0, waiting for transfers between devices: 84.6 us -> none  [local(): left_inverses = lax.all_gather(rounded[0][None], 'mp', axis=0, tiled=True)]
  transfers between devices with their start and end apart: 6 -> 6, of which waited for: 5 -> 5; matrix products, arithmetic and copies ran while one was open for 2% -> 3% of each run, Pallas kernels for 0% -> 0%
where the time goes in v1:
time: 874 us; the launch traced here: 873 us
  waiting for transfers between devices  645 us (74%)
  blocking collectives  145 us (17%)
  starting transfers between devices  20.9 us (2%)
  matrix products  19.6 us (2%)
  between operations  19.1 us (2%)
  other arithmetic  13.1 us (1%)
  local copies, waits for them, and re-layouts  9.84 us (1%)
    psum x1, waiting for transfers between devices, from_root(): return lax.psum(block, axis)  286 us
    psum x1, waiting for transfers between devices, local(): summed, totals = lax.psum((partials, counts.astype(jnp.float32)), 'dp')  202 us
    reduce_scatter x1, waiting for transfers between devices, local(): lax.psum_scatter(contract_rows(grads_kept, features), 'dp', scatter_dimen...  143 us
    psum x1, blocking collectives, local(): curvature = lax.psum(curvature, ('dp', 'mp'))  74.8 us
    psum x1, blocking collectives, local(): summed, totals = lax.psum((partials, counts.astype(jnp.float32)), 'dp')  70.3 us
  transfers between devices with their start and end apart: 6, of which 5 were waited for; matrix products, arithmetic and copies ran while one was open for 3% of the time, Pallas kernels for 0%

profile of v1, /device:TPU:1, one launch (start us, length us, event | category | flops | bytes accessed | tf_op | source)
XLA Modules:
  0.0 872.6 jit_solution(3656402731046754066)
XLA Ops:
  7.9 2.4 fusion.41
  10.3 2.4 fusion.44
  12.7 1.5 pad_maximum_fusion
  14.3 70.3 %psum.36 = f32[]{:T(128)} all-reduce(f32[]{:T(128)} %bitcast.12), channel_id=1, replica_groups=mesh['dp'=32,'mp'=8] {'dp'}, use_global_device_ids=true, to_apply=%region_1.2 | all-reduce | flops 1 | bytes 8 | tf_op jit(solution)/shard_map/psum | solution.py:46
  87.8 201.8 %all-reduce.4.cloned.1.call-done = f32[2,512,512]{2,1,0:T(8,128)} async-done(((f32[2,512,512]{2,1,0:T(8,128)}), f32[2,512,512]{2,1,0:T(8,128)}) %all-reduce.4.cloned.1.call-update) | async-done | bytes 2097168 | tf_op jit(solution)/shard_map/psum | solution.py:46
  289.6 1.2 conditional.3
  289.7 1.1 stack.33.clone
  290.8 2.8 maximum_select_fusion.1
  293.6 1.2 conditional.2
  294.9 2.8 maximum_select_fusion
  298.9 10.3 %fusion.37 = f32[512,4096]{1,0:T(8,128)} fusion(bf16[1024,4096]{1,0:T(8,128)(2,1)} %param.11, bf16[1024,512]{1,0:T(8,128)(2,1)S(1)} %copy-done.4, pred[1024]{0:T(1024)(128)(4,1)S(1)} %iota_compare_fusion.4), kind=kOutput, calls=%fused_computation.52 | convolution fusion | flops 4295491584 | bytes 17826816 | tf_op jit(solution)/shard_map/dot_general | solution.py:16
  309.2 286.5 %all-reduce.6.cloned.1.call-done = (f32[2,512,512]{2,1,0:T(8,128)}, f32[2,512,512]{2,1,0:T(8,128)}) async-done(((f32[2,512,512]{2,1,0:T(8,128)}, f32[2,512,512]{2,1,0:T(8,128)}), (f32[2,512,512]{2,1,0:T(8,128)}, f32[2,512,512]{2,1,0:T(8,128)})) %all-reduce.6.cloned.1.call-update) | async-done | bytes 4194320 | tf_op jit(solution)/shard_map/psum | solution.py:12
  595.6 1.3 fusion.62
  596.9 2.3 stack.46
  599.2 4.6 all-to-all-start
  605.6 143.3 %reduce-scatter.2.cloned.1.call-done = f32[16,4096]{1,0:T(8,128)} async-done(((f32[512,4096]{1,0:T(8,128)}), f32[16,4096]{1,0:T(8,128)}) %reduce-scatter.2.cloned.1.call-update) | async-done | bytes 262160 | tf_op jit(solution)/shard_map/reduce_scatter | solution.py:89
  749.9 1.6 copy_bitcast_fusion
  751.6 10.9 %all-to-all-start.2 = ((bf16[16,32,128]{2,0,1:T(8,128)(2,1)}), bf16[16,32,128]{2,0,1:T(8,128)(2,1)S(1)}, u32[]{:S(2)}, u32[]{:S(2)}) async-start(bf16[16,32,128]{2,0,1:T(8,128)(2,1)} %copy_bitcast_fusion), calls=%async_computation.3 | async-start | bytes 262144 | tf_op jit(solution)/shard_map/all_to_all | solution.py:100
  762.5 3.5 fusion.50
  766.9 6.1 all-to-all-done.2
  773.0 5.1 all-to-all-start.1
  778.2 3.4 select_bitcast_fusion
  781.5 7.3 all-to-all-done.1
  789.8 74.8 %psum.39 = f32[]{:T(128)} all-reduce(f32[]{:T(128)} %get-tuple-element.140), channel_id=1, replica_groups=mesh['dp'=32,'mp'=8] {'dp','mp'}, use_global_device_ids=true, to_apply=%region_10.11 | all-reduce | flops 1 | bytes 8 | tf_op jit(solution)/shard_map/psum | solution.py:105
  (31 shorter events, 7.4 us)
Async XLA Ops:
  7.2 282.4 %all-reduce.4.cloned.1.call-start = ((), (), s32[]{:S(2)}) async-start(), calls=%async_computation.4 | async-start | bytes 4194304 | tf_op jit(solution)/shard_map/psum | solution.py:46
  14.3 70.3 %copy-start.5 = (s32[8,2]{0,1:T(2,128)S(1)}, s32[8,2]{0,1:T(2,128)}, u32[]{:S(2)}) copy-start(s32[8,2]{0,1:T(2,128)} %param.16) | copy-start | bytes 196
  14.3 70.3 %copy-start.6 = (s32[8,2]{0,1:T(2,128)S(1)}, s32[8,2]{0,1:T(2,128)}, u32[]{:S(2)}) copy-start(s32[8,2]{0,1:T(2,128)} %param.17) | copy-start | bytes 196
  14.3 275.3 %copy-start = (f32[1,1,2,512,512]{4,3,2,1,0:T(8,128)S(1)}, f32[1,1,2,512,512]{4,3,2,1,0:T(8,128)}, u32[]{:S(2)}) copy-start(f32[1,1,2,512,512]{4,3,2,1,0:T(8,128)} %param.15) | copy-start | bytes 6291460
  14.3 581.4 %all-reduce.6.cloned.1.call-start = ((), (), s32[]{:S(2)}) async-start(), calls=%async_computation.6 | async-start | bytes 8388608 | tf_op jit(solution)/shard_map/psum | solution.py:12
  297.6 1.2 copy-start.4
  297.7 451.3 %reduce-scatter.2.cloned.1.call-start = ((), (), s32[]{:S(2)}) async-start(), calls=%async_computation.5 | async-start | bytes 8650752 | tf_op jit(solution)/shard_map/reduce_scatter | solution.py:89
  599.2 152.3 %all-to-all-start = ((bf16[8,1,512,512]{3,2,1,0:T(8,128)(2,1)}), bf16[8,1,512,512]{3,2,1,0:T(8,128)(2,1)}, u32[]{:S(2)}, u32[]{:S(2)}) async-start(bf16[8,1,512,512]{3,2,1,0:T(8,128)(2,1)} %stack.46), calls=%async_computation | async-start | bytes 8388608 | tf_op jit(solution)/shard_map/all_to_all | solution.py:80
  751.6 21.5 %all-to-all-start.2 = ((bf16[16,32,128]{2,0,1:T(8,128)(2,1)}), bf16[16,32,128]{2,0,1:T(8,128)(2,1)S(1)}, u32[]{:S(2)}, u32[]{:S(2)}) async-start(bf16[16,32,128]{2,0,1:T(8,128)(2,1)} %copy_bitcast_fusion), calls=%async_computation.3 | async-start | bytes 262144 | tf_op jit(solution)/shard_map/all_to_all | solution.py:100
  762.5 15.7 %copy-start.2 = (f32[2,512,512]{2,1,0:T(8,128)S(1)}, f32[2,512,512]{2,1,0:T(8,128)}, u32[]{:S(2)}) copy-start(f32[2,512,512]{2,1,0:T(8,128)} %get-tuple-element.133) | copy-start | bytes 6291460
  773.0 15.8 %all-to-all-start.1 = ((bf16[16,32,128]{2,0,1:T(8,128)(2,1)}), bf16[16,32,128]{2,0,1:T(8,128)(2,1)S(1)}, u32[]{:S(2)}, u32[]{:S(2)}) async-start(bf16[16,32,128]{2,0,1:T(8,128)(2,1)} %copy.29), calls=%async_computation.2 | async-start | bytes 262144 | tf_op jit(solution)/shard_map/all_to_all | solution.py:99
Sparse Core Ops, SparseCore 0:
  14.4 275.1 all-reduce.3
  297.8 297.8 all-reduce.5
  600.7 148.2 reduce-scatter.1
